TPU v7x, 32 devices: a whole 2x2x4 slice. The times are simulated.
32 devices in a mesh: groups: 2 (over y), ctx: 8 (over z, x), tp: 2 (over core).
Axes of the slice: x: 2, y: 2, z: 4, core: 2. Of those that a mesh axis runs over, the one named last changes fastest.
Arguments:
- queries: bfloat16 [2048, 2048], P(('groups', 'ctx'), 'tp'), parts along dimension 0, may hold values from -10 to 10
- keys: bfloat16 [2048, 512], P(('groups', 'ctx'), 'tp'), parts along dimension 0, may hold values from -10 to 10
- values: bfloat16 [2048, 512], P(('groups', 'ctx'), 'tp'), parts along dimension 0, may hold values from -6 to 6
- cotangent: bfloat16 [2048, 2048], P(('groups', 'ctx'), 'tp'), parts along dimension 0, may hold values from -6 to 6
- key_probe: bfloat16 [2048, 512], P(('groups', 'ctx'), 'tp'), parts along dimension 0, may hold values from -6 to 6
- value_probe: bfloat16 [2048, 512], P(('groups', 'ctx'), 'tp'), parts along dimension 0, may hold values from -6 to 6
- segments: int32 [2048], P(('groups', 'ctx')), parts along dimension 0, may hold values from 0 to 1, never falling along the last dimension, each value on 1 to 640 neighbouring positions
Outputs:
- hvp_keys: float32 [2048, 512], P(('groups', 'ctx'), 'tp'), parts along dimension 0
- hvp_values: float32 [2048, 512], P(('groups', 'ctx'), 'tp'), parts along dimension 0
There are 2 independent parts, one for each index of `groups`. A program takes and returns all parts, laid end to end along the dimension named above; each array names one. Nothing has to cross between parts.
Inputs may be any that keep to these rules, and one draw needn't show every extreme that they name: `segments`: document numbers never fall along the tokens; each document holds 1 to 640 tokens.
All inputs are finite; a program needn't handle non-finite values.
Results may differ from a plain program's by a relative error of at most 0.0029.
Values may be sent and summed in bfloat16 or wider, within the bound.
A program may use at most 64 MiB of HBM per device.

v0:
```python
import functools

import jax
import jax.numpy as jnp
from jax import lax
from jax.experimental import pallas as pl
from jax.experimental.pallas import tpu as pltpu
from jax.sharding import PartitionSpec as P

HEAD_WIDTH = 128
DOC = 640
LABEL_ROWS = 16
MESH = pl.DeviceIdType.MESH
SCALE = HEAD_WIDTH ** (-0.5)
LOG2E = 1.4426950408889634


def lowest_shard(shard, count, rows):
    total = count * rows
    slack = -(-total // DOC) * DOC - total
    margin = -(-slack // rows)
    per_doc = DOC // rows
    start = (shard // per_doc) * per_doc - margin
    if isinstance(shard, int):
        return max(0, start, shard - per_doc)
    return jnp.maximum(jnp.maximum(start, shard - per_doc), 0)


def kernel(count, reach, q_ref, c_ref, k_ref, v_ref, dk_ref, dv_ref, lab_ref, ok_ref, ov_ref,
           pack, inbox, qs, cs, prod, peaks, outbox, retbox, kv_send, kv_recv, ret_send, ret_recv):
    rows, kv_width = k_ref.shape
    heads = kv_width // HEAD_WIDTH
    group = q_ref.shape[1] // kv_width
    wide = group * rows
    me = lax.axis_index("ctx")
    lowest = functools.partial(lowest_shard, count=count, rows=rows)
    gives = [None] + [(me + d < count) & (lowest(me + d) <= me) for d in range(1, reach + 1)]
    takes = [None] + [me - d >= lowest(me) for d in range(1, reach + 1)]

    barrier = pltpu.get_barrier_semaphore()
    for d in range(1, reach + 1):
        @pl.when(gives[d])
        def _():
            pl.semaphore_signal(barrier, inc=1, device_id={"ctx": me + d}, device_id_type=MESH)

        @pl.when(takes[d])
        def _():
            pl.semaphore_signal(barrier, inc=1, device_id={"ctx": me - d}, device_id_type=MESH)

    pack[0:rows, :] = k_ref[...]
    pack[rows : 2 * rows, :] = dk_ref[...]
    pack[2 * rows : 3 * rows, :] = v_ref[...]
    pack[3 * rows : 4 * rows, :] = dv_ref[...]
    my_labels = lab_ref[...].astype(jnp.float32)
    label_rows = jnp.broadcast_to(my_labels, (LABEL_ROWS, rows)).astype(jnp.bfloat16)
    for h in range(kv_width // rows):
        pack[4 * rows :, h * rows : (h + 1) * rows] = label_rows
    partners = 0
    for d in range(1, reach + 1):
        partners = partners + gives[d].astype(jnp.int32) + takes[d].astype(jnp.int32)
    pl.semaphore_wait(barrier, partners)

    def kv_copy(d):
        return pltpu.make_async_remote_copy(
            src_ref=pack, dst_ref=inbox.at[d - 1], send_sem=kv_send.at[d - 1], recv_sem=kv_recv.at[d - 1],
            device_id={"ctx": me + d}, device_id_type=MESH)

    def ret_copy(d):
        return pltpu.make_async_remote_copy(
            src_ref=outbox.at[d - 1], dst_ref=retbox.at[d - 1], send_sem=ret_send.at[d - 1],
            recv_sem=ret_recv.at[d - 1], device_id={"ctx": me - d}, device_id_type=MESH)

    for d in range(1, reach + 1):
        @pl.when(gives[d])
        def _():
            kv_copy(d).start()

    for h in range(heads):
        for g in range(group):
            at = (h * group + g) * HEAD_WIDTH
            qs[h, g * rows : (g + 1) * rows, :] = q_ref[:, at : at + HEAD_WIDTH]
            cs[h, g * rows : (g + 1) * rows, :] = c_ref[:, at : at + HEAD_WIDTH]

    def absorb(d, block):
        their = jnp.broadcast_to(block[4 * rows : 4 * rows + 8, 0:rows].astype(jnp.float32)[0:1], (rows, rows))
        keep = their.T == my_labels
        if d == 0:
            keys = lax.broadcasted_iota(jnp.int32, (rows, rows), 0)
            asks = lax.broadcasted_iota(jnp.int32, (rows, rows), 1)
            keep = keep & (keys <= asks)
        nt = (((1,), (1,)), ((), ()))
        for h in range(heads):
            cols = slice(h * HEAD_WIDTH, (h + 1) * HEAD_WIDTH)
            prod[d, h, 0 : 2 * rows, :] = lax.dot_general(
                block[0 : 2 * rows, cols], qs[h], nt, preferred_element_type=jnp.float32)
            prod[d, h, 2 * rows : 4 * rows, :] = lax.dot_general(
                block[2 * rows : 4 * rows, cols], cs[h], nt, preferred_element_type=jnp.float32)
            for g in range(group):
                lanes = slice(g * rows, (g + 1) * rows)
                masked = jnp.where(keep, prod[d, h, 0:rows, lanes], -jnp.inf)
                top = jnp.max(masked, axis=0, keepdims=True)
                if d > 0:
                    old = peaks[h, 0:1, lanes]
                    top = jnp.maximum(top, old)
                    factor = jnp.exp2((old - top) * (SCALE * LOG2E))
                weight = jnp.exp2((masked - top) * (SCALE * LOG2E))
                prod[d, h, 0:rows, lanes] = weight
                slope = prod[d, h, rows : 2 * rows, lanes]
                along = prod[d, h, 2 * rows : 3 * rows, lanes]
                probed = prod[d, h, 3 * rows : 4 * rows, lanes]
                leaning = weight * slope
                sums = [weight, weight * along, leaning, leaning * along, weight * probed]
                for s, term in enumerate(sums):
                    term = jnp.sum(term, axis=0, keepdims=True)
                    if d > 0:
                        term = term + peaks[h, s + 1 : s + 2, lanes] * factor
                    peaks[h, s + 1 : s + 2, lanes] = term
                peaks[h, 0:1, lanes] = top
                peaks[h, 8 + d : 9 + d, lanes] = top

    absorb(0, pack)
    for d in range(1, reach + 1):
        @pl.when(takes[d])
        def _():
            kv_copy(d).wait_recv()
            absorb(d, inbox.at[d - 1])

    for h in range(heads):
        inverse = 1.0 / peaks[h, 1:2, :]
        mean_a = peaks[h, 2:3, :] * inverse
        mean_s = peaks[h, 3:4, :] * inverse
        mean_c = peaks[h, 4:5, :] * inverse
        mean_p = peaks[h, 5:6, :] * inverse
        peaks[h, 1:2, :] = inverse
        peaks[h, 2:3, :] = mean_a
        peaks[h, 4:5, :] = SCALE * (mean_c - mean_s * mean_a) + mean_p
        peaks[h, 3:4, :] = mean_s

    def terms(d, put):
        for h in range(heads):
            factor = jnp.exp2((peaks[h, 8 + d : 9 + d, :] - peaks[h, 0:1, :]) * (SCALE * LOG2E)) * peaks[h, 1:2, :]
            combined_parts, tangent_parts = [], []
            for g in range(group):
                lanes = slice(g * rows, (g + 1) * rows)
                probability = prod[d, h, 0:rows, lanes] * factor[:, lanes]
                tangent = probability * ((prod[d, h, rows : 2 * rows, lanes] - peaks[h, 3:4, lanes]) * SCALE)
                combined = (tangent * (prod[d, h, 2 * rows : 3 * rows, lanes] - peaks[h, 2:3, lanes])
                            + probability * (prod[d, h, 3 * rows : 4 * rows, lanes] - peaks[h, 4:5, lanes]))
                tangent_parts.append(tangent.astype(jnp.bfloat16))
                combined_parts.append(combined.astype(jnp.bfloat16))
            put(h, SCALE * jnp.dot(jnp.concatenate(combined_parts, axis=1), qs[h],
                                   preferred_element_type=jnp.float32),
                jnp.dot(jnp.concatenate(tangent_parts, axis=1), cs[h], preferred_element_type=jnp.float32))

    for d in range(reach, 0, -1):
        @pl.when(takes[d])
        def _():
            def put(h, key_term, value_term):
                cols = slice(h * HEAD_WIDTH, (h + 1) * HEAD_WIDTH)
                outbox[d - 1, 0:rows, cols] = key_term.astype(jnp.bfloat16)
                outbox[d - 1, rows : 2 * rows, cols] = value_term.astype(jnp.bfloat16)

            terms(d, put)
            ret_copy(d).start()

    def put_own(h, key_term, value_term):
        cols = slice(h * HEAD_WIDTH, (h + 1) * HEAD_WIDTH)
        ok_ref[:, cols] = key_term
        ov_ref[:, cols] = value_term

    terms(0, put_own)

    for d in range(1, reach + 1):
        @pl.when(gives[d])
        def _():
            ret_copy(d).wait_recv()
            ok_ref[...] += retbox[d - 1, 0:rows, :].astype(jnp.float32)
            ov_ref[...] += retbox[d - 1, rows : 2 * rows, :].astype(jnp.float32)

    for d in range(1, reach + 1):
        @pl.when(gives[d])
        def _():
            kv_copy(d).wait_send()

        @pl.when(takes[d])
        def _():
            ret_copy(d).wait_send()


def shards(queries, keys, values, cotangent, key_probe, value_probe, segments):
    rows, kv_width = keys.shape
    heads = kv_width // HEAD_WIDTH
    group = queries.shape[1] // kv_width
    count = lax.axis_size("ctx")
    reach = max(i - lowest_shard(i, count, rows) for i in range(count))
    packed = 4 * rows + LABEL_ROWS
    vmem = pl.BlockSpec(memory_space=pltpu.VMEM)
    shape = jax.ShapeDtypeStruct((rows, kv_width), jnp.float32)
    return pl.pallas_call(
        functools.partial(kernel, count, reach),
        out_shape=(shape, shape),
        in_specs=[vmem] * 7,
        out_specs=(vmem, vmem),
        scratch_shapes=[
            pltpu.VMEM((packed, kv_width), jnp.bfloat16),
            pltpu.VMEM((reach, packed, kv_width), jnp.bfloat16),
            pltpu.VMEM((heads, group * rows, HEAD_WIDTH), jnp.bfloat16),
            pltpu.VMEM((heads, group * rows, HEAD_WIDTH), jnp.bfloat16),
            pltpu.VMEM((reach + 1, heads, 4 * rows, group * rows), jnp.float32),
            pltpu.VMEM((heads, 16, group * rows), jnp.float32),
            pltpu.VMEM((reach, 2 * rows, kv_width), jnp.bfloat16),
            pltpu.VMEM((reach, 2 * rows, kv_width), jnp.bfloat16),
            pltpu.SemaphoreType.DMA((reach,)),
            pltpu.SemaphoreType.DMA((reach,)),
            pltpu.SemaphoreType.DMA((reach,)),
            pltpu.SemaphoreType.DMA((reach,)),
        ],
        compiler_params=pltpu.CompilerParams(
            collective_id=0, has_side_effects=True, vmem_limit_bytes=40 * 1024 * 1024),
        cost_estimate=pl.CostEstimate(flops=1_200_000_000, bytes_accessed=2_000_000, transcendentals=800_000),
    )(queries, cotangent, keys, values, key_probe, value_probe, segments.reshape(1, rows))


def solution(mesh):
    return jax.shard_map(
        shards,
        mesh=mesh,
        in_specs=(P(("groups", "ctx"), "tp"),) * 6 + (P(("groups", "ctx")),),
        out_specs=(P(("groups", "ctx"), "tp"), P(("groups", "ctx"), "tp")),
        check_vma=False,
    )
```

profile of v0, /device:TPU:18, one launch (start us, length us, event | category | flops | bytes accessed | tf_op | source)
XLA Modules:
  0.0 51.2 jit_solution(2856852778618935093)
XLA Ops:
  0.6 0.0 copy-start.6
  0.6 0.6 %copy-done.6 = s32[128]{0:T(128)S(1)} copy-done((s32[128]{0:T(128)S(1)}, s32[128]{0:T(128)}, u32[]{:S(2)}) %copy-start.6) | copy-done | bytes 536
  1.3 0.0 copy-start
  1.3 0.9 %copy-done = bf16[128,1024]{1,0:T(8,128)(2,1)S(1)} copy-done((bf16[128,1024]{1,0:T(8,128)(2,1)S(1)}, bf16[128,1024]{1,0:T(8,128)(2,1)}, u32[]{:S(2)}) %copy-start) | copy-done | bytes 262168
  2.2 0.0 copy-start.1
  2.2 0.9 %copy-done.1 = bf16[128,1024]{1,0:T(8,128)(2,1)S(1)} copy-done((bf16[128,1024]{1,0:T(8,128)(2,1)S(1)}, bf16[128,1024]{1,0:T(8,128)(2,1)}, u32[]{:S(2)}) %copy-start.1) | copy-done | bytes 262168
  3.2 0.0 copy-start.2
  3.2 0.8 %copy-done.2 = bf16[128,256]{1,0:T(8,128)(2,1)S(1)} copy-done((bf16[128,256]{1,0:T(8,128)(2,1)S(1)}, bf16[128,256]{1,0:T(8,128)(2,1)}, u32[]{:S(2)}) %copy-start.2) | copy-done | bytes 65560
  4.0 0.0 copy-start.3
  4.0 0.8 %copy-done.3 = bf16[128,256]{1,0:T(8,128)(2,1)S(1)} copy-done((bf16[128,256]{1,0:T(8,128)(2,1)S(1)}, bf16[128,256]{1,0:T(8,128)(2,1)}, u32[]{:S(2)}) %copy-start.3) | copy-done | bytes 65560
  4.9 0.0 copy-start.4
  4.9 0.8 %copy-done.4 = bf16[128,256]{1,0:T(8,128)(2,1)S(1)} copy-done((bf16[128,256]{1,0:T(8,128)(2,1)S(1)}, bf16[128,256]{1,0:T(8,128)(2,1)}, u32[]{:S(2)}) %copy-start.4) | copy-done | bytes 65560
  5.7 0.0 copy-start.5
  5.7 0.8 %copy-done.5 = bf16[128,256]{1,0:T(8,128)(2,1)S(1)} copy-done((bf16[128,256]{1,0:T(8,128)(2,1)S(1)}, bf16[128,256]{1,0:T(8,128)(2,1)}, u32[]{:S(2)}) %copy-start.5) | copy-done | bytes 65560
  6.5 43.3 %shard_map.86 = (f32[128,256]{1,0:T(8,128)S(1)}, f32[128,256]{1,0:T(8,128)S(1)}) custom-call(bf16[128,1024]{1,0:T(8,128)(2,1)S(1)} %copy-done, bf16[128,1024]{1,0:T(8,128)(2,1)S(1)} %copy-done.1, bf16[128,256]{1,0:T(8,128)(2,1)S(1)} %copy-done.2, bf16[128,256]{1,0:T(8,128)(2,1)S(1)} %copy-done.3, bf16[128,256]{1,0:T(8,128)(2,1)S(1)} %copy-done.4, ...), custom_call_target="tpu_custom_call" | custom-call | flops 1200000000 | bytes 2000000 | tf_op jit(solution)/shard_map/pallas_call | solution.py:199
  49.8 0.7 %copy.11 = f32[128,256]{1,0:T(8,128)} copy(f32[128,256]{1,0:T(8,128)S(1)} %get-tuple-element.4) | data formatting | bytes 262144
  50.5 0.7 %copy.12 = f32[128,256]{1,0:T(8,128)} copy(f32[128,256]{1,0:T(8,128)S(1)} %get-tuple-element.5) | data formatting | bytes 262144
Async XLA Ops:
  0.6 0.7 %copy-start.6 = (s32[128]{0:T(128)S(1)}, s32[128]{0:T(128)}, u32[]{:S(2)}) copy-start(s32[128]{0:T(128)} %param.13) | copy-start | bytes 1540
  1.3 0.9 %copy-start = (bf16[128,1024]{1,0:T(8,128)(2,1)S(1)}, bf16[128,1024]{1,0:T(8,128)(2,1)}, u32[]{:S(2)}) copy-start(bf16[128,1024]{1,0:T(8,128)(2,1)} %q_ref.1) | copy-start | bytes 786436
  2.2 0.9 %copy-start.1 = (bf16[128,1024]{1,0:T(8,128)(2,1)S(1)}, bf16[128,1024]{1,0:T(8,128)(2,1)}, u32[]{:S(2)}) copy-start(bf16[128,1024]{1,0:T(8,128)(2,1)} %c_ref.1) | copy-start | bytes 786436
  3.2 0.8 %copy-start.2 = (bf16[128,256]{1,0:T(8,128)(2,1)S(1)}, bf16[128,256]{1,0:T(8,128)(2,1)}, u32[]{:S(2)}) copy-start(bf16[128,256]{1,0:T(8,128)(2,1)} %k_ref.1) | copy-start | bytes 196612
  4.0 0.8 %copy-start.3 = (bf16[128,256]{1,0:T(8,128)(2,1)S(1)}, bf16[128,256]{1,0:T(8,128)(2,1)}, u32[]{:S(2)}) copy-start(bf16[128,256]{1,0:T(8,128)(2,1)} %v_ref.1) | copy-start | bytes 196612
  4.9 0.8 %copy-start.4 = (bf16[128,256]{1,0:T(8,128)(2,1)S(1)}, bf16[128,256]{1,0:T(8,128)(2,1)}, u32[]{:S(2)}) copy-start(bf16[128,256]{1,0:T(8,128)(2,1)} %dk_ref.1) | copy-start | bytes 196612
  5.7 0.8 %copy-start.5 = (bf16[128,256]{1,0:T(8,128)(2,1)S(1)}, bf16[128,256]{1,0:T(8,128)(2,1)}, u32[]{:S(2)}) copy-start(bf16[128,256]{1,0:T(8,128)(2,1)} %dv_ref.1) | copy-start | bytes 196612
where the time goes:
time: 51.5 us; the launch traced here: 51.2 us
  Pallas kernels  43.3 us (84%)
  local copies, waits for them, and re-layouts  7.22 us (14%)
  between operations  0.66 us (1%)
    pallas_call x1, Pallas kernels, shards(): pl.pallas_call(functools.partial(kernel, count, reach), out_shape=(shape,...  43.3 us
    unnamed x16, local copies, waits for them, and re-layouts  7.22 us

commit v1 on v0

v1 whole, which is shorter than its diff:
```python
import functools

import jax
import jax.numpy as jnp
from jax import lax
from jax.experimental import pallas as pl
from jax.experimental.pallas import tpu as pltpu
from jax.sharding import PartitionSpec as P

HEAD_WIDTH = 128
DOC = 640
LABEL_ROWS = 16
MESH = pl.DeviceIdType.MESH
SCALE = HEAD_WIDTH ** (-0.5)
LOG2E = 1.4426950408889634


def lowest_shard(shard, count, rows):
    total = count * rows
    slack = -(-total // DOC) * DOC - total
    margin = -(-slack // rows)
    per_doc = DOC // rows
    start = (shard // per_doc) * per_doc - margin
    if isinstance(shard, int):
        return max(0, start, shard - per_doc)
    return jnp.maximum(jnp.maximum(start, shard - per_doc), 0)


ROUTES = (
    (0, None, 0, 2), (0, None, 0, 1), (0, None, 2, 4), (0, 0, 2, 3), (0, 1, 1, 3),
    (1, None, 1, 3), (1, None, 3, 2), (1, None, 3, 5), (1, None, 5, 4),
    (2, None, 2, 4), (2, None, 2, 3),
    (3, None, 3, 5), (3, None, 5, 7), (3, None, 5, 4), (3, None, 7, 6),
    (4, None, 4, 6), (4, None, 4, 5), (4, None, 6, 7),
    (5, None, 5, 7), (5, None, 7, 6),
    (6, None, 6, 7),
)


class Edge:
    def __init__(self, h, a, b, holders, gives):
        self.h, self.a, self.b, self.holders, self.gives = h, a, b, holders, gives

    def sends(self, me):
        if self.holders is None:
            return self.gives(me)
        found = me == self.holders[0]
        for other in self.holders[1:]:
            found = found | (me == other)
        return found

    def receives(self, me):
        step = self.b - self.a
        if self.holders is None:
            return (me >= step) & self.gives(me - step)
        found = me == self.holders[0] + step
        for other in self.holders[1:]:
            found = found | (me == other + step)
        return found


def edges_of(count, rows, heads, reach):
    lowest = functools.partial(lowest_shard, count=count, rows=rows)
    reached = {(j, i) for i in range(count) for j in range(lowest(i), i)}
    routed = {(j, t) for j, _, _, t in ROUTES}
    result = []
    if count == 8 and reached <= routed and DOC // rows == 5:
        table = {}
        for owner, part, start, end in ROUTES:
            for h in range(heads):
                if part is None or h % 2 == part:
                    table.setdefault((h, start - owner, end - owner), []).append(start)
        for (h, a, b), holders in table.items():
            result.append(Edge(h, a, b, holders, None))
    else:
        for d in range(1, reach + 1):
            for h in range(heads):
                result.append(Edge(h, 0, d, None, lambda me, d=d: (me + d < count) & (lowest(me + d) <= me)))
    return result


def either(flags):
    found = flags[0]
    for flag in flags[1:]:
        found = found | flag
    return found


def kernel(count, reach, edges, q_ref, c_ref, k_ref, v_ref, dk_ref, dv_ref, lab_ref, ok_ref, ov_ref,
           labels, pack, inbox, qs, cs, prod, peaks, acc, outbox, retbox,
           load_sem, kv_send, kv_recv, ret_send, ret_recv):
    rows, kv_width = k_ref.shape
    heads = kv_width // HEAD_WIDTH
    group = q_ref.shape[1] // kv_width
    me = lax.axis_index("ctx")
    takes = [None] + [me - d >= lowest_shard(me, count, rows) for d in range(1, reach + 1)]
    sends = [e.sends(me) for e in edges]
    receives = [e.receives(me) for e in edges]
    into = {(d, h): [n for n, e in enumerate(edges) if (e.b, e.h) == (d, h)]
            for d in range(1, reach + 1) for h in range(heads)}
    out_of = {(d, h): [n for n, e in enumerate(edges) if (e.a, e.h) == (d, h)]
              for d in range(reach + 1) for h in range(heads)}

    loads = [pltpu.make_async_copy(lab_ref, labels, load_sem.at[0])]
    for h in range(heads):
        cols = slice(h * HEAD_WIDTH, (h + 1) * HEAD_WIDTH)
        for n, ref in enumerate((k_ref, dk_ref, v_ref, dv_ref)):
            loads.append(pltpu.make_async_copy(
                ref.at[:, cols], pack.at[h, n * rows : (n + 1) * rows, :], load_sem.at[len(loads)]))
    first = len(loads)
    for h in range(heads):
        for g in range(group):
            at = (h * group + g) * HEAD_WIDTH
            for ref, to in ((q_ref, qs), (c_ref, cs)):
                loads.append(pltpu.make_async_copy(
                    ref.at[:, at : at + HEAD_WIDTH], to.at[h, g * rows : (g + 1) * rows, :],
                    load_sem.at[len(loads)]))
    for load in loads:
        load.start()

    barrier = pltpu.get_barrier_semaphore()
    partners = 0
    for step in sorted({e.b - e.a for e in edges}):
        up = either([sends[n] for n, e in enumerate(edges) if e.b - e.a == step])
        down = either([receives[n] for n, e in enumerate(edges) if e.b - e.a == step])

        @pl.when(up)
        def _():
            pl.semaphore_signal(barrier, inc=1, device_id={"ctx": me + step}, device_id_type=MESH)

        @pl.when(down)
        def _():
            pl.semaphore_signal(barrier, inc=1, device_id={"ctx": me - step}, device_id_type=MESH)

        partners = partners + up.astype(jnp.int32) + down.astype(jnp.int32)

    for load in loads[:first]:
        load.wait()
    my_labels = labels[...].astype(jnp.float32)
    for h in range(heads):
        pack[h, 4 * rows :, :] = jnp.broadcast_to(my_labels, (LABEL_ROWS, rows)).astype(jnp.bfloat16)
    pl.semaphore_wait(barrier, partners)

    def kv_copy(n):
        e = edges[n]
        return pltpu.make_async_remote_copy(
            src_ref=pack.at[e.h] if e.a == 0 else inbox.at[e.a - 1, e.h], dst_ref=inbox.at[e.b - 1, e.h],
            send_sem=kv_send.at[n], recv_sem=kv_recv.at[e.b - 1, e.h],
            device_id={"ctx": me + (e.b - e.a)}, device_id_type=MESH)

    def ret_copy(n):
        e = edges[n]
        return pltpu.make_async_remote_copy(
            src_ref=outbox.at[e.b - 1, e.h], dst_ref=retbox.at[n], send_sem=ret_send.at[n],
            recv_sem=ret_recv.at[n], device_id={"ctx": me - (e.b - e.a)}, device_id_type=MESH)

    def pass_on(d, h):
        for n in out_of[d, h]:
            @pl.when(sends[n])
            def _():
                kv_copy(n).start()

    for h in range(heads):
        pass_on(0, h)
    for load in loads[first:]:
        load.wait()

    def absorb(d, h, block):
        their = jnp.broadcast_to(block[4 * rows : 4 * rows + 8, :].astype(jnp.float32)[0:1], (rows, rows))
        keep = their.T == my_labels
        if d == 0:
            keys = lax.broadcasted_iota(jnp.int32, (rows, rows), 0)
            asks = lax.broadcasted_iota(jnp.int32, (rows, rows), 1)
            keep = keep & (keys <= asks)
        nt = (((1,), (1,)), ((), ()))
        prod[d, h, 0 : 2 * rows, :] = lax.dot_general(
            block[0 : 2 * rows, :], qs[h], nt, preferred_element_type=jnp.float32)
        prod[d, h, 2 * rows : 4 * rows, :] = lax.dot_general(
            block[2 * rows : 4 * rows, :], cs[h], nt, preferred_element_type=jnp.float32)
        for g in range(group):
            lanes = slice(g * rows, (g + 1) * rows)
            masked = jnp.where(keep, prod[d, h, 0:rows, lanes], -jnp.inf)
            top = jnp.max(masked, axis=0, keepdims=True)
            if d > 0:
                old = peaks[h, 0:1, lanes]
                top = jnp.maximum(top, old)
                factor = jnp.exp2((old - top) * (SCALE * LOG2E))
            weight = jnp.exp2((masked - top) * (SCALE * LOG2E))
            prod[d, h, 0:rows, lanes] = weight
            slope = prod[d, h, rows : 2 * rows, lanes]
            along = prod[d, h, 2 * rows : 3 * rows, lanes]
            probed = prod[d, h, 3 * rows : 4 * rows, lanes]
            leaning = weight * slope
            sums = [weight, weight * along, leaning, leaning * along, weight * probed]
            for s, term in enumerate(sums):
                term = jnp.sum(term, axis=0, keepdims=True)
                if d > 0:
                    term = term + peaks[h, s + 1 : s + 2, lanes] * factor
                peaks[h, s + 1 : s + 2, lanes] = term
            peaks[h, 0:1, lanes] = top
            peaks[h, 8 + d : 9 + d, lanes] = top

    for h in range(heads):
        absorb(0, h, pack.at[h])
    order = [d for d in (2, 1, 4, 3) if d <= reach] + list(range(5, reach + 1))
    for d in order:
        for h in range(heads):
            if into[d, h]:
                @pl.when(either([receives[n] for n in into[d, h]]))
                def _():
                    kv_copy(into[d, h][0]).wait_recv()
                    pass_on(d, h)

                @pl.when(takes[d])
                def _():
                    absorb(d, h, inbox.at[d - 1, h])

    for h in range(heads):
        inverse = 1.0 / peaks[h, 1:2, :]
        mean_a = peaks[h, 2:3, :] * inverse
        mean_s = peaks[h, 3:4, :] * inverse
        mean_c = peaks[h, 4:5, :] * inverse
        mean_p = peaks[h, 5:6, :] * inverse
        peaks[h, 1:2, :] = inverse
        peaks[h, 2:3, :] = mean_a
        peaks[h, 4:5, :] = SCALE * (mean_c - mean_s * mean_a) + mean_p
        peaks[h, 3:4, :] = mean_s

    def terms(d, h):
        factor = jnp.exp2((peaks[h, 8 + d : 9 + d, :] - peaks[h, 0:1, :]) * (SCALE * LOG2E)) * peaks[h, 1:2, :]
        combined_parts, tangent_parts = [], []
        for g in range(group):
            lanes = slice(g * rows, (g + 1) * rows)
            probability = prod[d, h, 0:rows, lanes] * factor[:, lanes]
            tangent = probability * ((prod[d, h, rows : 2 * rows, lanes] - peaks[h, 3:4, lanes]) * SCALE)
            combined = (tangent * (prod[d, h, 2 * rows : 3 * rows, lanes] - peaks[h, 2:3, lanes])
                        + probability * (prod[d, h, 3 * rows : 4 * rows, lanes] - peaks[h, 4:5, lanes]))
            tangent_parts.append(tangent.astype(jnp.bfloat16))
            combined_parts.append(combined.astype(jnp.bfloat16))
        acc[d, h, 0:rows, :] = SCALE * jnp.dot(
            jnp.concatenate(combined_parts, axis=1), qs[h], preferred_element_type=jnp.float32)
        acc[d, h, rows : 2 * rows, :] = jnp.dot(
            jnp.concatenate(tangent_parts, axis=1), cs[h], preferred_element_type=jnp.float32)

    def give_back(d, h):
        outbox[d - 1, h] = acc[d, h].astype(jnp.bfloat16)
        for n in into[d, h]:
            @pl.when(receives[n])
            def _():
                ret_copy(n).start()

    back = [3, 4, 2, 1] if reach == 4 else list(range(reach, 0, -1))
    for d in back:
        for h in range(heads):
            if into[d, h]:
                @pl.when(takes[d])
                def _():
                    terms(d, h)

                passed = either([receives[n] for n in into[d, h]])
                inner = out_of[d, h] and either([sends[n] for n in out_of[d, h]])
                leaf = passed & ~inner if out_of[d, h] else passed

                @pl.when(leaf)
                def _():
                    give_back(d, h)

    for h in range(heads):
        terms(0, h)

    for d in back + [0]:
        for h in range(heads):
            if not out_of[d, h]:
                continue
            if d > 0:
                inner = either([sends[n] for n in out_of[d, h]])

                @pl.when(inner & ~takes[d])
                def _():
                    acc[d, h] = jnp.zeros_like(acc[d, h])

            for n in out_of[d, h]:
                @pl.when(sends[n])
                def _():
                    ret_copy(n).wait_recv()
                    acc[d, h] += retbox[n].astype(jnp.float32)

            if d > 0:
                @pl.when(inner)
                def _():
                    give_back(d, h)

    for h in range(heads):
        cols = slice(h * HEAD_WIDTH, (h + 1) * HEAD_WIDTH)
        ok_ref[:, cols] = acc[0, h, 0:rows, :]
        ov_ref[:, cols] = acc[0, h, rows : 2 * rows, :]

    for n in range(len(edges)):
        @pl.when(sends[n])
        def _():
            kv_copy(n).wait_send()

        @pl.when(receives[n])
        def _():
            ret_copy(n).wait_send()


def shards(queries, keys, values, cotangent, key_probe, value_probe, segments):
    rows, kv_width = keys.shape
    heads = kv_width // HEAD_WIDTH
    group = queries.shape[1] // kv_width
    count = lax.axis_size("ctx")
    reach = max(i - lowest_shard(i, count, rows) for i in range(count))
    edges = edges_of(count, rows, heads, reach)
    packed = 4 * rows + LABEL_ROWS
    vmem = pl.BlockSpec(memory_space=pltpu.VMEM)
    hbm = pl.BlockSpec(memory_space=pltpu.HBM)
    shape = jax.ShapeDtypeStruct((rows, kv_width), jnp.float32)
    return pl.pallas_call(
        functools.partial(kernel, count, reach, edges),
        out_shape=(shape, shape),
        in_specs=[hbm] * 7,
        out_specs=(vmem, vmem),
        scratch_shapes=[
            pltpu.VMEM((1, rows), jnp.int32),
            pltpu.VMEM((heads, packed, HEAD_WIDTH), jnp.bfloat16),
            pltpu.VMEM((reach, heads, packed, HEAD_WIDTH), jnp.bfloat16),
            pltpu.VMEM((heads, group * rows, HEAD_WIDTH), jnp.bfloat16),
            pltpu.VMEM((heads, group * rows, HEAD_WIDTH), jnp.bfloat16),
            pltpu.VMEM((reach + 1, heads, 4 * rows, group * rows), jnp.float32),
            pltpu.VMEM((heads, 16, group * rows), jnp.float32),
            pltpu.VMEM((reach + 1, heads, 2 * rows, HEAD_WIDTH), jnp.float32),
            pltpu.VMEM((reach, heads, 2 * rows, HEAD_WIDTH), jnp.bfloat16),
            pltpu.VMEM((len(edges), 2 * rows, HEAD_WIDTH), jnp.bfloat16),
            pltpu.SemaphoreType.DMA((1 + heads * (4 + 2 * group),)),
            pltpu.SemaphoreType.DMA((len(edges),)),
            pltpu.SemaphoreType.DMA((reach, heads)),
            pltpu.SemaphoreType.DMA((len(edges),)),
            pltpu.SemaphoreType.DMA((len(edges),)),
        ],
        compiler_params=pltpu.CompilerParams(
            collective_id=0, has_side_effects=True, vmem_limit_bytes=40 * 1024 * 1024),
        cost_estimate=pl.CostEstimate(flops=1_200_000_000, bytes_accessed=2_000_000, transcendentals=800_000),
    )(queries, cotangent, keys, values, key_probe, value_probe, segments.reshape(1, rows))


def solution(mesh):
    return jax.shard_map(
        shards,
        mesh=mesh,
        in_specs=(P(("groups", "ctx"), "tp"),) * 6 + (P(("groups", "ctx")),),
        out_specs=(P(("groups", "ctx"), "tp"), P(("groups", "ctx"), "tp")),
        check_vma=False,
    )
```

time: 51.5 us -> 42.5 us (0.83)
  the two profiles are of different devices: /device:TPU:18 before, /device:TPU:6 now
where the time goes in v1:
time: 42.5 us; the launch traced here: 42.2 us
  Pallas kernels  34.3 us (81%)
  local copies, waits for them, and re-layouts  7.22 us (17%)
  between operations  0.66 us (2%)
    pallas_call x1, Pallas kernels, shards(): pl.pallas_call(functools.partial(kernel, count, reach, edges), out_shape=...  34.3 us
    unnamed x16, local copies, waits for them, and re-layouts  7.22 us

profile of v1, /device:TPU:6, one launch (start us, length us, event | category | flops | bytes accessed | tf_op | source)
XLA Modules:
  0.0 42.2 jit_solution(8517881413582420824)
XLA Ops:
  0.6 0.0 copy-start.6
  0.6 0.6 %copy-done.6 = s32[128]{0:T(128)S(1)} copy-done((s32[128]{0:T(128)S(1)}, s32[128]{0:T(128)}, u32[]{:S(2)}) %copy-start.6) | copy-done | bytes 536
  1.3 0.0 copy-start
  1.3 0.9 %copy-done = bf16[128,1024]{1,0:T(8,128)(2,1)S(1)} copy-done((bf16[128,1024]{1,0:T(8,128)(2,1)S(1)}, bf16[128,1024]{1,0:T(8,128)(2,1)}, u32[]{:S(2)}) %copy-start) | copy-done | bytes 262168
  2.2 0.0 copy-start.1
  2.2 0.9 %copy-done.1 = bf16[128,1024]{1,0:T(8,128)(2,1)S(1)} copy-done((bf16[128,1024]{1,0:T(8,128)(2,1)S(1)}, bf16[128,1024]{1,0:T(8,128)(2,1)}, u32[]{:S(2)}) %copy-start.1) | copy-done | bytes 262168
  3.2 0.0 copy-start.2
  3.2 0.8 %copy-done.2 = bf16[128,256]{1,0:T(8,128)(2,1)S(1)} copy-done((bf16[128,256]{1,0:T(8,128)(2,1)S(1)}, bf16[128,256]{1,0:T(8,128)(2,1)}, u32[]{:S(2)}) %copy-start.2) | copy-done | bytes 65560
  4.0 0.0 copy-start.3
  4.0 0.8 %copy-done.3 = bf16[128,256]{1,0:T(8,128)(2,1)S(1)} copy-done((bf16[128,256]{1,0:T(8,128)(2,1)S(1)}, bf16[128,256]{1,0:T(8,128)(2,1)}, u32[]{:S(2)}) %copy-start.3) | copy-done | bytes 65560
  4.9 0.0 copy-start.4
  4.9 0.8 %copy-done.4 = bf16[128,256]{1,0:T(8,128)(2,1)S(1)} copy-done((bf16[128,256]{1,0:T(8,128)(2,1)S(1)}, bf16[128,256]{1,0:T(8,128)(2,1)}, u32[]{:S(2)}) %copy-start.4) | copy-done | bytes 65560
  5.7 0.0 copy-start.5
  5.7 0.8 %copy-done.5 = bf16[128,256]{1,0:T(8,128)(2,1)S(1)} copy-done((bf16[128,256]{1,0:T(8,128)(2,1)S(1)}, bf16[128,256]{1,0:T(8,128)(2,1)}, u32[]{:S(2)}) %copy-start.5) | copy-done | bytes 65560
  6.5 34.3 %shard_map.86 = (f32[128,256]{1,0:T(8,128)S(1)}, f32[128,256]{1,0:T(8,128)S(1)}) custom-call(bf16[128,1024]{1,0:T(8,128)(2,1)S(1)} %copy-done, bf16[128,1024]{1,0:T(8,128)(2,1)S(1)} %copy-done.1, bf16[128,256]{1,0:T(8,128)(2,1)S(1)} %copy-done.2, bf16[128,256]{1,0:T(8,128)(2,1)S(1)} %copy-done.3, bf16[128,256]{1,0:T(8,128)(2,1)S(1)} %copy-done.4, ...), custom_call_target="tpu_custom_call" | custom-call | flops 1200000000 | bytes 2000000 | tf_op jit(solution)/shard_map/pallas_call | solution.py:319
  40.9 0.7 %copy.11 = f32[128,256]{1,0:T(8,128)} copy(f32[128,256]{1,0:T(8,128)S(1)} %get-tuple-element.4) | data formatting | bytes 262144
  41.5 0.7 %copy.12 = f32[128,256]{1,0:T(8,128)} copy(f32[128,256]{1,0:T(8,128)S(1)} %get-tuple-element.5) | data formatting | bytes 262144
Async XLA Ops:
  0.6 0.7 %copy-start.6 = (s32[128]{0:T(128)S(1)}, s32[128]{0:T(128)}, u32[]{:S(2)}) copy-start(s32[128]{0:T(128)} %param.13) | copy-start | bytes 1540
  1.3 0.9 %copy-start = (bf16[128,1024]{1,0:T(8,128)(2,1)S(1)}, bf16[128,1024]{1,0:T(8,128)(2,1)}, u32[]{:S(2)}) copy-start(bf16[128,1024]{1,0:T(8,128)(2,1)} %q_ref.1) | copy-start | bytes 786436
  2.2 0.9 %copy-start.1 = (bf16[128,1024]{1,0:T(8,128)(2,1)S(1)}, bf16[128,1024]{1,0:T(8,128)(2,1)}, u32[]{:S(2)}) copy-start(bf16[128,1024]{1,0:T(8,128)(2,1)} %c_ref.1) | copy-start | bytes 786436
  3.2 0.8 %copy-start.2 = (bf16[128,256]{1,0:T(8,128)(2,1)S(1)}, bf16[128,256]{1,0:T(8,128)(2,1)}, u32[]{:S(2)}) copy-start(bf16[128,256]{1,0:T(8,128)(2,1)} %k_ref.1) | copy-start | bytes 196612
  4.0 0.8 %copy-start.3 = (bf16[128,256]{1,0:T(8,128)(2,1)S(1)}, bf16[128,256]{1,0:T(8,128)(2,1)}, u32[]{:S(2)}) copy-start(bf16[128,256]{1,0:T(8,128)(2,1)} %v_ref.1) | copy-start | bytes 196612
  4.9 0.8 %copy-start.4 = (bf16[128,256]{1,0:T(8,128)(2,1)S(1)}, bf16[128,256]{1,0:T(8,128)(2,1)}, u32[]{:S(2)}) copy-start(bf16[128,256]{1,0:T(8,128)(2,1)} %dk_ref.1) | copy-start | bytes 196612
  5.7 0.8 %copy-start.5 = (bf16[128,256]{1,0:T(8,128)(2,1)S(1)}, bf16[128,256]{1,0:T(8,128)(2,1)}, u32[]{:S(2)}) copy-start(bf16[128,256]{1,0:T(8,128)(2,1)} %dv_ref.1) | copy-start | bytes 196612

commit v2 on v1

--- a/solution.py
+++ b/solution.py
@@ -30,11 +30,12 @@
     (0, None, 0, 2), (0, None, 0, 1), (0, None, 2, 4), (0, 0, 2, 3), (0, 1, 1, 3),
     (1, None, 1, 3), (1, None, 3, 2), (1, None, 3, 5), (1, None, 5, 4),
     (2, None, 2, 4), (2, None, 2, 3),
-    (3, None, 3, 5), (3, None, 5, 7), (3, None, 5, 4), (3, None, 7, 6),
+    (3, None, 3, 5), (3, None, 5, 4), (3, None, 5, 7), (3, None, 4, 6),
     (4, None, 4, 6), (4, None, 4, 5), (4, None, 6, 7),
     (5, None, 5, 7), (5, None, 7, 6),
     (6, None, 6, 7),
 )
+RETURNS = tuple(r for r in ROUTES if r != (3, None, 4, 6)) + ((3, None, 7, 6),)
 
 
 class Edge:
@@ -59,14 +60,14 @@
         return found
 
 
-def edges_of(count, rows, heads, reach):
+def edges_of(routes, count, rows, heads, reach):
     lowest = functools.partial(lowest_shard, count=count, rows=rows)
     reached = {(j, i) for i in range(count) for j in range(lowest(i), i)}
-    routed = {(j, t) for j, _, _, t in ROUTES}
+    routed = {(j, t) for j, _, _, t in routes}
     result = []
     if count == 8 and reached <= routed and DOC // rows == 5:
         table = {}
-        for owner, part, start, end in ROUTES:
+        for owner, part, start, end in routes:
             for h in range(heads):
                 if part is None or h % 2 == part:
                     table.setdefault((h, start - owner, end - owner), []).append(start)
@@ -86,7 +87,7 @@
     return found
 
 
-def kernel(count, reach, edges, q_ref, c_ref, k_ref, v_ref, dk_ref, dv_ref, lab_ref, ok_ref, ov_ref,
+def kernel(count, reach, edges, redges, q_ref, c_ref, k_ref, v_ref, dk_ref, dv_ref, lab_ref, ok_ref, ov_ref,
            labels, pack, inbox, qs, cs, prod, peaks, acc, outbox, retbox,
            load_sem, kv_send, kv_recv, ret_send, ret_recv):
     rows, kv_width = k_ref.shape
@@ -94,19 +95,22 @@
     group = q_ref.shape[1] // kv_width
     me = lax.axis_index("ctx")
     takes = [None] + [me - d >= lowest_shard(me, count, rows) for d in range(1, reach + 1)]
+    units = [(d, h) for d in range(reach + 1) for h in range(heads)]
     sends = [e.sends(me) for e in edges]
     receives = [e.receives(me) for e in edges]
-    into = {(d, h): [n for n, e in enumerate(edges) if (e.b, e.h) == (d, h)]
-            for d in range(1, reach + 1) for h in range(heads)}
-    out_of = {(d, h): [n for n, e in enumerate(edges) if (e.a, e.h) == (d, h)]
-              for d in range(reach + 1) for h in range(heads)}
+    into = {u: [n for n, e in enumerate(edges) if (e.b, e.h) == u] for u in units}
+    out_of = {u: [n for n, e in enumerate(edges) if (e.a, e.h) == u] for u in units}
+    adds = [e.sends(me) for e in redges]
+    yields = [e.receives(me) for e in redges]
+    parents = {u: [n for n, e in enumerate(redges) if (e.b, e.h) == u] for u in units}
+    children = {u: [n for n, e in enumerate(redges) if (e.a, e.h) == u] for u in units}
 
     loads = [pltpu.make_async_copy(lab_ref, labels, load_sem.at[0])]
     for h in range(heads):
         cols = slice(h * HEAD_WIDTH, (h + 1) * HEAD_WIDTH)
         for n, ref in enumerate((k_ref, dk_ref, v_ref, dv_ref)):
             loads.append(pltpu.make_async_copy(
-                ref.at[:, cols], pack.at[h, n * rows : (n + 1) * rows, :], load_sem.at[len(loads)]))
+                ref.at[:, cols], pack.at[h, LABEL_ROWS + n * rows : LABEL_ROWS + (n + 1) * rows, :], load_sem.at[len(loads)]))
     first = len(loads)
     for h in range(heads):
         for g in range(group):
@@ -120,53 +124,55 @@
 
     barrier = pltpu.get_barrier_semaphore()
     partners = 0
-    for step in sorted({e.b - e.a for e in edges}):
-        up = either([sends[n] for n, e in enumerate(edges) if e.b - e.a == step])
-        down = either([receives[n] for n, e in enumerate(edges) if e.b - e.a == step])
+    both = [(e, x, y) for e, x, y in zip(edges + redges, sends + adds, receives + yields)]
+    forth = [(e.b - e.a, x) for e, x, _ in both] + [(e.a - e.b, y) for e, _, y in both]
+    for step in sorted({step for step, _ in forth}):
+        up = either([flag for other, flag in forth if other == step])
 
         @pl.when(up)
         def _():
             pl.semaphore_signal(barrier, inc=1, device_id={"ctx": me + step}, device_id_type=MESH)
 
-        @pl.when(down)
-        def _():
-            pl.semaphore_signal(barrier, inc=1, device_id={"ctx": me - step}, device_id_type=MESH)
-
-        partners = partners + up.astype(jnp.int32) + down.astype(jnp.int32)
+        partners = partners + up.astype(jnp.int32)
 
     for load in loads[:first]:
         load.wait()
     my_labels = labels[...].astype(jnp.float32)
     for h in range(heads):
-        pack[h, 4 * rows :, :] = jnp.broadcast_to(my_labels, (LABEL_ROWS, rows)).astype(jnp.bfloat16)
+        pack[h, 0:LABEL_ROWS, :] = jnp.broadcast_to(my_labels, (LABEL_ROWS, rows)).astype(jnp.bfloat16)
     pl.semaphore_wait(barrier, partners)
 
-    def kv_copy(n):
+    middle = LABEL_ROWS + 2 * rows
+    cuts = (slice(0, middle), slice(middle, middle + 2 * rows))
+
+    def kv_copy(n, c):
         e = edges[n]
+        block = pack.at[e.h] if e.a == 0 else inbox.at[e.a - 1, e.h]
         return pltpu.make_async_remote_copy(
-            src_ref=pack.at[e.h] if e.a == 0 else inbox.at[e.a - 1, e.h], dst_ref=inbox.at[e.b - 1, e.h],
-            send_sem=kv_send.at[n], recv_sem=kv_recv.at[e.b - 1, e.h],
+            src_ref=block.at[cuts[c]], dst_ref=inbox.at[e.b - 1, e.h, cuts[c]],
+            send_sem=kv_send.at[n, c], recv_sem=kv_recv.at[e.b - 1, e.h, c],
             device_id={"ctx": me + (e.b - e.a)}, device_id_type=MESH)
 
     def ret_copy(n):
-        e = edges[n]
+        e = redges[n]
         return pltpu.make_async_remote_copy(
             src_ref=outbox.at[e.b - 1, e.h], dst_ref=retbox.at[n], send_sem=ret_send.at[n],
             recv_sem=ret_recv.at[n], device_id={"ctx": me - (e.b - e.a)}, device_id_type=MESH)
 
-    def pass_on(d, h):
+    def pass_on(d, h, c):
         for n in out_of[d, h]:
             @pl.when(sends[n])
             def _():
-                kv_copy(n).start()
-
-    for h in range(heads):
-        pass_on(0, h)
+                kv_copy(n, c).start()
+
+    for h in range(heads):
+        for c in range(2):
+            pass_on(0, h, c)
     for load in loads[first:]:
         load.wait()
 
     def absorb(d, h, block):
-        their = jnp.broadcast_to(block[4 * rows : 4 * rows + 8, :].astype(jnp.float32)[0:1], (rows, rows))
+        their = jnp.broadcast_to(block[0:LABEL_ROWS, :].astype(jnp.float32)[0:1], (rows, rows))
         keep = their.T == my_labels
         if d == 0:
             keys = lax.broadcasted_iota(jnp.int32, (rows, rows), 0)
@@ -174,9 +180,9 @@
             keep = keep & (keys <= asks)
         nt = (((1,), (1,)), ((), ()))
         prod[d, h, 0 : 2 * rows, :] = lax.dot_general(
-            block[0 : 2 * rows, :], qs[h], nt, preferred_element_type=jnp.float32)
+            block[cuts[0].start + LABEL_ROWS : middle, :], qs[h], nt, preferred_element_type=jnp.float32)
         prod[d, h, 2 * rows : 4 * rows, :] = lax.dot_general(
-            block[2 * rows : 4 * rows, :], cs[h], nt, preferred_element_type=jnp.float32)
+            block[middle : middle + 2 * rows, :], cs[h], nt, preferred_element_type=jnp.float32)
         for g in range(group):
             lanes = slice(g * rows, (g + 1) * rows)
             masked = jnp.where(keep, prod[d, h, 0:rows, lanes], -jnp.inf)
@@ -208,8 +214,9 @@
             if into[d, h]:
                 @pl.when(either([receives[n] for n in into[d, h]]))
                 def _():
-                    kv_copy(into[d, h][0]).wait_recv()
-                    pass_on(d, h)
+                    for c in range(2):
+                        kv_copy(into[d, h][0], c).wait_recv()
+                        pass_on(d, h, c)
 
                 @pl.when(takes[d])
                 def _():
@@ -244,22 +251,22 @@
 
     def give_back(d, h):
         outbox[d - 1, h] = acc[d, h].astype(jnp.bfloat16)
-        for n in into[d, h]:
-            @pl.when(receives[n])
+        for n in parents[d, h]:
+            @pl.when(yields[n])
             def _():
                 ret_copy(n).start()
 
     back = [3, 4, 2, 1] if reach == 4 else list(range(reach, 0, -1))
     for d in back:
         for h in range(heads):
-            if into[d, h]:
+            if parents[d, h]:
                 @pl.when(takes[d])
                 def _():
                     terms(d, h)
 
-                passed = either([receives[n] for n in into[d, h]])
-                inner = out_of[d, h] and either([sends[n] for n in out_of[d, h]])
-                leaf = passed & ~inner if out_of[d, h] else passed
+                leaf = either([yields[n] for n in parents[d, h]])
+                if children[d, h]:
+                    leaf = leaf & ~either([adds[n] for n in children[d, h]])
 
                 @pl.when(leaf)
                 def _():
@@ -270,17 +277,17 @@
 
     for d in back + [0]:
         for h in range(heads):
-            if not out_of[d, h]:
+            if not children[d, h]:
                 continue
             if d > 0:
-                inner = either([sends[n] for n in out_of[d, h]])
+                inner = either([adds[n] for n in children[d, h]])
 
                 @pl.when(inner & ~takes[d])
                 def _():
                     acc[d, h] = jnp.zeros_like(acc[d, h])
 
-            for n in out_of[d, h]:
-                @pl.when(sends[n])
+            for n in children[d, h]:
+                @pl.when(adds[n])
                 def _():
                     ret_copy(n).wait_recv()
                     acc[d, h] += retbox[n].astype(jnp.float32)
@@ -298,9 +305,11 @@
     for n in range(len(edges)):
         @pl.when(sends[n])
         def _():
-            kv_copy(n).wait_send()
-
-        @pl.when(receives[n])
+            for c in range(2):
+                kv_copy(n, c).wait_send()
+
+    for n in range(len(redges)):
+        @pl.when(yields[n])
         def _():
             ret_copy(n).wait_send()
 
@@ -311,13 +320,14 @@
     group = queries.shape[1] // kv_width
     count = lax.axis_size("ctx")
     reach = max(i - lowest_shard(i, count, rows) for i in range(count))
-    edges = edges_of(count, rows, heads, reach)
+    edges = edges_of(ROUTES, count, rows, heads, reach)
+    redges = edges_of(RETURNS, count, rows, heads, reach)
     packed = 4 * rows + LABEL_ROWS
     vmem = pl.BlockSpec(memory_space=pltpu.VMEM)
     hbm = pl.BlockSpec(memory_space=pltpu.HBM)
     shape = jax.ShapeDtypeStruct((rows, kv_width), jnp.float32)
     return pl.pallas_call(
-        functools.partial(kernel, count, reach, edges),
+        functools.partial(kernel, count, reach, edges, redges),
         out_shape=(shape, shape),
         in_specs=[hbm] * 7,
         out_specs=(vmem, vmem),
@@ -331,15 +341,15 @@
             pltpu.VMEM((heads, 16, group * rows), jnp.float32),
             pltpu.VMEM((reach + 1, heads, 2 * rows, HEAD_WIDTH), jnp.float32),
             pltpu.VMEM((reach, heads, 2 * rows, HEAD_WIDTH), jnp.bfloat16),
-            pltpu.VMEM((len(edges), 2 * rows, HEAD_WIDTH), jnp.bfloat16),
+            pltpu.VMEM((len(redges), 2 * rows, HEAD_WIDTH), jnp.bfloat16),
             pltpu.SemaphoreType.DMA((1 + heads * (4 + 2 * group),)),
-            pltpu.SemaphoreType.DMA((len(edges),)),
-            pltpu.SemaphoreType.DMA((reach, heads)),
-            pltpu.SemaphoreType.DMA((len(edges),)),
-            pltpu.SemaphoreType.DMA((len(edges),)),
+            pltpu.SemaphoreType.DMA((len(edges), 2)),
+            pltpu.SemaphoreType.DMA((reach, heads, 2)),
+            pltpu.SemaphoreType.DMA((len(redges),)),
+            pltpu.SemaphoreType.DMA((len(redges),)),
         ],
         compiler_params=pltpu.CompilerParams(
-            collective_id=0, has_side_effects=True, vmem_limit_bytes=40 * 1024 * 1024),
+            collective_id=0, has_side_effects=True, vmem_limit_bytes=64 * 1024 * 1024 - 64 * 1024),
         cost_estimate=pl.CostEstimate(flops=1_200_000_000, bytes_accessed=2_000_000, transcendentals=800_000),
     )(queries, cotangent, keys, values, key_probe, value_probe, segments.reshape(1, rows))
 

time: 42.5 us -> 36.4 us (0.86)
  local copies, waits for them, and re-layouts: 7.22 us -> 2.26 us
  Pallas kernels: 34.3 us -> 33.2 us
    unnamed x16 -> x4, local copies, waits for them, and re-layouts: 7.22 us -> 2.26 us
    pallas_call x1, Pallas kernels: 34.3 us -> 33.2 us  [shards(): pl.pallas_call(functools.partial(kernel, count, reach, edges, redges), ou...]
where the time goes in v2:
time: 36.4 us; the launch traced here: 36.2 us
  Pallas kernels  33.2 us (91%)
  local copies, waits for them, and re-layouts  2.26 us (6%)
  between operations  0.65 us (2%)
    pallas_call x1, Pallas kernels, shards(): pl.pallas_call(functools.partial(kernel, count, reach, edges, redges), ou...  33.2 us
    unnamed x4, local copies, waits for them, and re-layouts  2.26 us

profile of v2, /device:TPU:6, one launch (start us, length us, event | category | flops | bytes accessed | tf_op | source)
XLA Modules:
  0.0 36.2 jit_solution(5093850238228762183)
XLA Ops:
  0.6 33.2 %shard_map.86 = (f32[128,256]{1,0:T(8,128)}, f32[128,256]{1,0:T(8,128)}) custom-call(bf16[128,1024]{1,0:T(8,128)(2,1)} %q_ref.1, bf16[128,1024]{1,0:T(8,128)(2,1)} %c_ref.1, bf16[128,256]{1,0:T(8,128)(2,1)} %k_ref.1, bf16[128,256]{1,0:T(8,128)(2,1)} %v_ref.1, bf16[128,256]{1,0:T(8,128)(2,1)} %dk_ref.1, bf16[128,256]{1,0:T(8,128)(2,1)} %dv_ref.1, ...), custom_call_target="tpu_custom_call" | custom-call | flops 1200000000 | bytes 2000000 | tf_op jit(solution)/shard_map/pallas_call | solution.py:329
  33.9 0.0 copy-start
  33.9 1.6 %copy.11 = f32[128,256]{1,0:T(8,128)} copy(f32[128,256]{1,0:T(8,128)} %get-tuple-element.4) | data formatting | bytes 262144
  35.5 0.0 copy-done
  35.5 0.7 %copy.12 = f32[128,256]{1,0:T(8,128)} copy(f32[128,256]{1,0:T(8,128)S(1)} %copy-done) | data formatting | bytes 262144
Async XLA Ops:
  33.9 1.6 %copy-start = (f32[128,256]{1,0:T(8,128)S(1)}, f32[128,256]{1,0:T(8,128)}, u32[]{:S(2)}) copy-start(f32[128,256]{1,0:T(8,128)} %get-tuple-element.5) | copy-start | bytes 393220

commit v3 on v2

--- a/solution.py
+++ b/solution.py
@@ -35,7 +35,15 @@
     (5, None, 5, 7), (5, None, 7, 6),
     (6, None, 6, 7),
 )
-RETURNS = tuple(r for r in ROUTES if r != (3, None, 4, 6)) + ((3, None, 7, 6),)
+RETURNS = (
+    (0, None, 0, 2), (0, None, 0, 1), (0, None, 0, 4), (0, 0, 2, 3), (0, 1, 1, 3),
+    (1, None, 1, 3), (1, None, 3, 2), (1, None, 1, 5), (1, None, 5, 4),
+    (2, None, 2, 4), (2, None, 2, 3),
+    (3, None, 3, 5), (3, None, 5, 7), (3, None, 5, 4), (3, None, 7, 6),
+    (4, None, 4, 6), (4, None, 4, 5), (4, None, 6, 7),
+    (5, None, 5, 7), (5, None, 7, 6),
+    (6, None, 6, 7),
+)
 
 
 class Edge:
@@ -87,7 +95,7 @@
     return found
 
 
-def kernel(count, reach, edges, redges, q_ref, c_ref, k_ref, v_ref, dk_ref, dv_ref, lab_ref, ok_ref, ov_ref,
+def kernel(count, reach, edges, redges, q_ref, c_ref, k_ref, v_ref, dk_ref, dv_ref, lab_ref, out_ref,
            labels, pack, inbox, qs, cs, prod, peaks, acc, outbox, retbox,
            load_sem, kv_send, kv_recv, ret_send, ret_recv):
     rows, kv_width = k_ref.shape
@@ -299,8 +307,8 @@
 
     for h in range(heads):
         cols = slice(h * HEAD_WIDTH, (h + 1) * HEAD_WIDTH)
-        ok_ref[:, cols] = acc[0, h, 0:rows, :]
-        ov_ref[:, cols] = acc[0, h, rows : 2 * rows, :]
+        out_ref[0:rows, cols] = acc[0, h, 0:rows, :]
+        out_ref[rows : 2 * rows, cols] = acc[0, h, rows : 2 * rows, :]
 
     for n in range(len(edges)):
         @pl.when(sends[n])
@@ -325,12 +333,12 @@
     packed = 4 * rows + LABEL_ROWS
     vmem = pl.BlockSpec(memory_space=pltpu.VMEM)
     hbm = pl.BlockSpec(memory_space=pltpu.HBM)
-    shape = jax.ShapeDtypeStruct((rows, kv_width), jnp.float32)
-    return pl.pallas_call(
+    shape = jax.ShapeDtypeStruct((2 * rows, kv_width), jnp.float32)
+    both = pl.pallas_call(
         functools.partial(kernel, count, reach, edges, redges),
-        out_shape=(shape, shape),
+        out_shape=shape,
         in_specs=[hbm] * 7,
-        out_specs=(vmem, vmem),
+        out_specs=vmem,
         scratch_shapes=[
             pltpu.VMEM((1, rows), jnp.int32),
             pltpu.VMEM((heads, packed, HEAD_WIDTH), jnp.bfloat16),
@@ -352,6 +360,7 @@
             collective_id=0, has_side_effects=True, vmem_limit_bytes=64 * 1024 * 1024 - 64 * 1024),
         cost_estimate=pl.CostEstimate(flops=1_200_000_000, bytes_accessed=2_000_000, transcendentals=800_000),
     )(queries, cotangent, keys, values, key_probe, value_probe, segments.reshape(1, rows))
+    return both[:rows], both[rows:]
 
 
 def solution(mesh):

time: 36.4 us -> 33.8 us (0.929)
  the two profiles are of different devices: /device:TPU:6 before, /device:TPU:10 now
where the time goes in v3:
time: 33.8 us; the launch traced here: 33.5 us
  Pallas kernels  31.2 us (92%)
  local copies, waits for them, and re-layouts  1.69 us (5%)
  between operations  0.64 us (2%)
    pallas_call x1, Pallas kernels, shards(): pl.pallas_call(functools.partial(kernel, count, reach, edges, redges), ou...  31.2 us
    slice x1, local copies, waits for them, and re-layouts, shards(): return (both[:rows], both[rows:])  1.69 us

profile of v3, /device:TPU:10, one launch (start us, length us, event | category | flops | bytes accessed | tf_op | source)
XLA Modules:
  0.0 33.5 jit_solution(10041765010188039967)
XLA Ops:
  0.6 31.2 %shard_map.86 = f32[256,256]{1,0:T(8,128)} custom-call(bf16[128,1024]{1,0:T(8,128)(2,1)} %q_ref.1, bf16[128,1024]{1,0:T(8,128)(2,1)} %c_ref.1, bf16[128,256]{1,0:T(8,128)(2,1)} %k_ref.1, bf16[128,256]{1,0:T(8,128)(2,1)} %v_ref.1, bf16[128,256]{1,0:T(8,128)(2,1)} %dk_ref.1, bf16[128,256]{1,0:T(8,128)(2,1)} %dv_ref.1, s32[1,128]{1,0:T(1,128)} %bitcast.1), custom_call_target="tpu_custom_call" | custom-call | flops 1200000000 | bytes 2000000 | tf_op jit(solution)/shard_map/pallas_call | solution.py:337
  31.9 1.7 %fusion = (f32[128,256]{1,0:T(8,128)}, f32[128,256]{1,0:T(8,128)}) fusion(f32[256,256]{1,0:T(8,128)} %shard_map.86), kind=kLoop, calls=%fused_computation | loop fusion | bytes 524288 | tf_op jit(solution)/shard_map/slice | solution.py:363
